TPU v7x, 32 devices: a whole 2x2x4 slice. The times are simulated.
32 devices in a mesh: groups: 2 (over y), blocks: 16 (over z, x, core).
Axes of the slice: x: 2, y: 2, z: 4, core: 2. Of those that a mesh axis runs over, the one named last changes fastest.
Arguments:
- snapshot: bfloat16 [2, 128, 32, 512], P('groups', 'blocks'), parts along dimension 0, may hold values from -6 to 6
- cotangent: bfloat16 [2, 128, 32, 512], P('groups', 'blocks'), parts along dimension 0, may hold values from -6 to 6
- first_weight: bfloat16 [32, 864], replicated, may hold values from -0.21875 to 0.21875
- second_weight: bfloat16 [32, 864], replicated, may hold values from -0.21875 to 0.21875
- face_codes: int32 [32, 2], P(('groups', 'blocks')), parts along dimension 0, may hold values from 0 to 3, as said below
Outputs:
- input_grad: float32 [2, 128, 32, 512], P('groups', 'blocks'), parts along dimension 0
- first_update: float32 [64, 864], P('groups'), parts along dimension 0
- second_update: float32 [64, 864], P('groups'), parts along dimension 0
There are 2 independent parts, one for each index of `groups`. A program takes and returns all parts, laid end to end along the dimension named above; an argument that names none is the same for every part. Nothing has to cross between parts.
Inputs may be any that keep to these rules, and one draw needn't show every extreme that they name: face_codes[b, 1] equals face_codes[(b + 1) mod 16, 0]: both blocks of an interface carry the same code.
All inputs are finite; a program needn't handle non-finite values.
Results may differ from a plain program's by a relative error of at most 0.003.
Values may be sent and summed in bfloat16 or wider, within the bound.
A program may use at most 64 MiB of HBM per device.

v0:
```python
import jax
import jax.numpy as jnp
from jax import lax
from jax.sharding import PartitionSpec as P

R_CELLS = 32


def shifted_2(value, axis, steps):
    count = lax.axis_size(axis)
    pairs = [(source, (source + steps) % count) for source in range(count)]
    return lax.ppermute(value, axis, pairs)


def flip_plane(plane, code, radial, vertical):
    batch_count = plane.shape[0]
    channels = plane.shape[1]
    grid = plane.reshape(batch_count, channels, radial, vertical)
    grid = jnp.where(code % 2 == 1, grid[:, :, ::-1, :], grid)
    grid = jnp.where(code // 2 == 1, grid[:, :, :, ::-1], grid)
    return grid.reshape(batch_count, channels, radial * vertical)


def shifted(field, step_r, step_z, vertical):
    cells = field.shape[-1]
    margin = vertical + 1
    widths = [(0, 0)] * (field.ndim - 1) + [(margin, margin)]
    wide = jnp.pad(field, widths)
    offset = margin + (step_r - 1) * vertical + (step_z - 1)
    piece = lax.slice_in_dim(wide, offset, offset + cells, axis=field.ndim - 1)
    place = lax.broadcasted_iota(jnp.int32, (cells,), 0) % vertical + step_z - 1
    valid = (place >= 0) & (place < vertical)
    return jnp.where(valid, piece, jnp.zeros((), field.dtype))


def neighbor_planes(field):
    count = field.shape[1]
    from_lower = shifted_2(field[:, count - 1], "blocks", 1)
    from_upper = shifted_2(field[:, 0], "blocks", -1)
    return (from_lower, from_upper)


def padded_field(field, codes, radial, vertical):
    from_lower, from_upper = neighbor_planes(field)
    lower = flip_plane(from_lower, codes[0], radial, vertical)
    upper = flip_plane(from_upper, codes[1], radial, vertical)
    return jnp.concatenate([lower[:, None], field, upper[:, None]], axis=1)


def zero_padded(field):
    return jnp.pad(field, ((0, 0), (1, 1), (0, 0), (0, 0)))


def convolve(padded, weight, count, vertical):
    channels = padded.shape[2]
    total = None
    for step_r in range(3):
        for step_z in range(3):
            moved = shifted(padded, step_r, step_z, vertical)
            for step_a in range(3):
                tap_index = 9 * step_a + 3 * step_r + step_z
                kernel = weight[:, tap_index * channels : (tap_index + 1) * channels]
                term = jnp.einsum(
                    "oc,bacp->baop",
                    kernel,
                    moved[:, step_a : step_a + count],
                    preferred_element_type=jnp.float32,
                )
                total = term if total is None else total + term
    return total


def weight_gradient(padded, cotan, vertical):
    count = cotan.shape[1]
    found = {}
    for step_r in range(3):
        for step_z in range(3):
            moved = shifted(padded, step_r, step_z, vertical)
            for step_a in range(3):
                tap_index = 9 * step_a + 3 * step_r + step_z
                found[tap_index] = jnp.einsum(
                    "baop,bacp->oc",
                    cotan,
                    moved[:, step_a : step_a + count],
                    preferred_element_type=jnp.float32,
                )
    return jnp.concatenate([found[index] for index in range(27)], axis=1)


def plane_adjoint(plane, weight, step_a, vertical):
    channels = weight.shape[1] // 27
    total = None
    for step_r in range(3):
        for step_z in range(3):
            tap_index = 9 * step_a + 3 * step_r + step_z
            kernel = weight[:, tap_index * channels : (tap_index + 1) * channels]
            piece = shifted(plane, 2 - step_r, 2 - step_z, vertical)
            term = jnp.einsum("oc,bop->bcp", kernel, piece, preferred_element_type=jnp.float32)
            total = term if total is None else total + term
    return total


def adjoint(cotan, weight, codes, radial, vertical):
    count = cotan.shape[1]
    out_channels = weight.shape[0]
    channels = weight.shape[1] // 27
    reversed_weight = weight.reshape(out_channels, 27, channels)[:, ::-1, :]
    reversed_weight = reversed_weight.transpose(2, 1, 0).reshape(channels, 27 * out_channels)
    interior = convolve(zero_padded(cotan), reversed_weight, count, vertical)
    own_lower = flip_plane(
        plane_adjoint(cotan[:, 0], weight, 0, vertical), codes[0], radial, vertical
    )
    own_upper = flip_plane(
        plane_adjoint(cotan[:, count - 1], weight, 2, vertical), codes[1], radial, vertical
    )
    lower_add = shifted_2(own_upper, "blocks", 1)
    upper_add = shifted_2(own_lower, "blocks", -1)
    interior = interior.at[:, 0].add(lower_add)
    return interior.at[:, count - 1].add(upper_add)


def normalize(grad):
    return grad / jnp.sqrt(jnp.mean(grad * grad) + 1e-06)


def body(snapshot, cotangent, first_weight, second_weight, face_codes):
    count = snapshot.shape[1]
    radial = R_CELLS
    vertical = snapshot.shape[3] // radial
    codes = face_codes[0]
    field_padded = padded_field(snapshot, codes, radial, vertical)
    pre = convolve(field_padded, first_weight, count, vertical)
    hidden = jax.nn.silu(pre).astype(jnp.bfloat16)
    hidden_padded = padded_field(hidden, codes, radial, vertical)
    second_grad = weight_gradient(hidden_padded, cotangent, vertical)
    hidden_grad = adjoint(cotangent, second_weight, codes, radial, vertical)
    sigmoid_part = jax.nn.sigmoid(pre)
    pre_grad = (hidden_grad * sigmoid_part * (1.0 + pre * (1.0 - sigmoid_part))).astype(
        jnp.bfloat16
    )
    first_grad = weight_gradient(field_padded, pre_grad, vertical)
    first_total, second_total = lax.psum((first_grad, second_grad), "blocks")
    input_grad = cotangent.astype(jnp.float32) + adjoint(
        pre_grad, first_weight, codes, radial, vertical
    )
    return (input_grad, normalize(first_total), normalize(second_total))


def solution(mesh):
    return jax.shard_map(
        body,
        mesh=mesh,
        in_specs=(
            P("groups", "blocks", None, None),
            P("groups", "blocks", None, None),
            P(),
            P(),
            P(("groups", "blocks"), None),
        ),
        out_specs=(P("groups", "blocks", None, None), P("groups", None), P("groups", None)),
        check_vma=False,
    )
```

profile of v0, /device:TPU:0, one launch (start us, length us, event | category | flops | bytes accessed | tf_op | source)
XLA Modules:
  0.0 207.1 jit_solution(6006155757848173578)
XLA Ops:
  7.2 0.8 fusion.446
  8.2 5.5 %collective-permute-start.3 = (bf16[1,32,512]{1,2,0:T(8,128)(2,1)S(1)}, bf16[1,32,512]{1,2,0:T(8,128)(2,1)S(1)}, u32[]{:S(2)}, u32[]{:S(2)}) collective-permute-start(bf16[1,32,512]{1,2,0:T(8,128)(2,1)S(1)} %bitcast.1333), channel_id=1, source_target_pairs={{0,15},{1,0},{2,1},{3,2},{4,3},{5,4},{6,5},{7,6},{8,7},{9,8},{10,9... | collective-permute-start | bytes 98312 | tf_op jit(solution)/shard_map/ppermute | solution.py:12
  13.8 0.6 copy-done.7
  14.4 0.6 fusion.447
  17.7 0.8 copy-done.3
  21.0 3.9 %collective-permute-start.1 = (f32[1,32,512]{2,1,0:T(8,128)S(1)}, f32[1,32,512]{2,1,0:T(8,128)S(1)}, u32[]{:S(2)}, u32[]{:S(2)}) collective-permute-start(f32[1,32,512]{2,1,0:T(8,128)S(1)} %copy.14), channel_id=1, source_target_pairs={{0,15},{1,0},{2,1},{3,2},{4,3},{5,4},{6,5},{7,6},{8,7},{9,8},{10,9... | collective-permute-start | bytes 196616 | tf_op jit(solution)/shard_map/ppermute | solution.py:12
  30.6 0.6 copy.10
  31.4 0.6 copy-done
  32.4 0.6 copy.19
  33.8 0.8 copy-done.6
  34.6 1.9 fusion.54
  43.4 0.3 convolution_add_fusion.36
  45.4 0.3 convolution_add_fusion.29
  47.6 0.3 convolution_add_fusion.21
  49.4 0.3 fusion.1
  49.7 0.5 fusion.14
  50.5 0.6 multiply_convert_fusion
  56.9 4.7 %collective-permute-start.7 = (bf16[1,32,512]{2,1,0:T(8,128)(2,1)S(1)}, bf16[1,32,512]{2,1,0:T(8,128)(2,1)S(1)}, u32[]{:S(2)}, u32[]{:S(2)}) collective-permute-start(bf16[1,32,512]{2,1,0:T(8,128)(2,1)S(1)} %get-tuple-element.112), channel_id=1, source_target_pairs={{0,15},{1,0},{2,1},{3,2},{4,3},{5,4},{6,5},{7,6},{8,7},{9,8},{10,9... | collective-permute-start | bytes 98312 | tf_op jit(solution)/shard_map/ppermute | solution.py:12
  66.3 0.7 copy.23
  67.4 0.7 copy.21
  68.4 0.8 concatenate.37
  70.2 0.8 convolution_bitcast_fusion.46
  71.1 0.8 convolution_bitcast_fusion.55
  71.9 1.8 fusion.62
  73.7 0.8 convolution_bitcast_fusion.34
  74.5 0.8 convolution_bitcast_fusion.43
  75.3 0.8 convolution_bitcast_fusion.52
  76.1 0.8 convolution_bitcast_fusion.40
  76.9 0.8 convolution_bitcast_fusion.49
  77.7 0.8 convolution_bitcast_fusion.58
  78.5 0.8 convolution_bitcast_fusion.35
  79.3 0.8 convolution_bitcast_fusion.44
  80.1 0.8 convolution_bitcast_fusion.53
  80.9 0.8 convolution_bitcast_fusion.38
  81.8 0.8 convolution_bitcast_fusion.47
  82.6 0.8 convolution_bitcast_fusion.56
  83.4 0.8 convolution_bitcast_fusion.41
  84.2 0.8 convolution_bitcast_fusion.50
  85.0 0.8 convolution_bitcast_fusion.59
  85.8 0.8 convolution_bitcast_fusion.36
  86.6 0.8 convolution_bitcast_fusion.45
  87.4 0.8 convolution_bitcast_fusion.54
  88.2 0.8 convolution_bitcast_fusion.39
  89.0 0.8 convolution_bitcast_fusion.48
  89.8 0.8 convolution_bitcast_fusion.57
  90.6 0.8 convolution_bitcast_fusion.33
  91.4 0.8 convolution_bitcast_fusion.42
  92.2 0.8 convolution_bitcast_fusion.51
  94.5 1.1 convolution_bitcast_fusion.3
  95.6 1.0 convolution_bitcast_fusion.4
  96.6 1.1 convolution_bitcast_fusion.5
  100.0 0.3 convolution_add_fusion.6
  101.6 1.1 convolution_bitcast_fusion.9
  102.6 1.1 fusion
  103.7 1.8 concatenate.39
  105.5 2.1 %fusion.38 = f32[1,8,32,512]{3,2,1,0:T(8,128)S(1)} fusion(f32[1,8,32,512]{3,2,1,0:T(8,128)S(1)} %convolution_bitcast_fusion, f32[1,8,32,512]{3,2,1,0:T(8,128)S(1)} %convolution_bitcast_fusion.1, f32[1,8,32,512]{3,2,1,0:T(8,128)S(1)} %convolution_bitcast_fusion.2, f32[1,8,32,512]{3,2,1,0:T(8,128)} %convolution_bitcast_fusion.3, ...), kind=kOutput, calls=%fused_computation.116 | convolution fusion | flops 9830400 | bytes 6561792 | tf_op jit(solution)/shard_map/oc,bacp->baop/dot_general | solution.py:63
  107.7 0.9 fusion.133
  108.6 0.9 fusion.132
  109.4 0.9 convert_add_fusion
  110.3 84.8 %all-reduce.13.cloned.1.call-done = (f32[32,864]{1,0:T(8,128)}, f32[32,864]{1,0:T(8,128)}) async-done(((f32[32,864]{1,0:T(8,128)}, f32[32,864]{1,0:T(8,128)}), (f32[32,864]{1,0:T(8,128)}, f32[32,864]{1,0:T(8,128)})) %all-reduce.13.cloned.1.call-update) | async-done | bytes 221200 | tf_op jit(solution)/shard_map/psum | solution.py:142
  195.1 1.6 multiply_reduce_fusion
  197.3 0.6 multiply_reduce_fusion.1
  198.7 0.7 broadcast_divide_fusion.1
  199.6 0.7 broadcast_divide_fusion
  (212 shorter events, 36.6 us)
Async XLA Ops:
  7.2 10.5 %copy-start.1 = (bf16[1,8,32,512]{3,2,1,0:T(8,128)(2,1)S(1)}, bf16[1,8,32,512]{3,2,1,0:T(8,128)(2,1)}, u32[]{:S(2)}) copy-start(bf16[1,8,32,512]{3,2,1,0:T(8,128)(2,1)} %param.14) | copy-start | bytes 786436
  7.2 187.9 %all-reduce.13.cloned.1.call-start = ((), (), s32[]{:S(2)}) async-start(), calls=%async_computation | async-start | bytes 458752 | tf_op jit(solution)/shard_map/psum | solution.py:142
  8.2 25.1 %collective-permute-start.3 = (bf16[1,32,512]{1,2,0:T(8,128)(2,1)S(1)}, bf16[1,32,512]{1,2,0:T(8,128)(2,1)S(1)}, u32[]{:S(2)}, u32[]{:S(2)}) collective-permute-start(bf16[1,32,512]{1,2,0:T(8,128)(2,1)S(1)} %bitcast.1333), channel_id=1, source_target_pairs={{0,15},{1,0},{2,1},{3,2},{4,3},{5,4},{6,5},{7,6},{8,7},{9,8},{10,9... | collective-permute-start | bytes 98312 | tf_op jit(solution)/shard_map/ppermute | solution.py:12
  13.8 0.7 copy-start.7
  13.8 19.7 %collective-permute-start.2 = (bf16[1,32,512]{1,2,0:T(8,128)(2,1)S(1)}, bf16[1,32,512]{1,2,0:T(8,128)(2,1)S(1)}, u32[]{:S(2)}, u32[]{:S(2)}) collective-permute-start(bf16[1,32,512]{1,2,0:T(8,128)(2,1)S(1)} %bitcast.1332), channel_id=1, source_target_pairs={{0,1},{1,2},{2,3},{3,4},{4,5},{5,6},{6,7},{7,8},{8,9},{9,10},{10,1... | collective-permute-start | bytes 98312 | tf_op jit(solution)/shard_map/ppermute | solution.py:12
  17.7 0.8 copy-start.3
  21.0 29.4 %collective-permute-start.1 = (f32[1,32,512]{2,1,0:T(8,128)S(1)}, f32[1,32,512]{2,1,0:T(8,128)S(1)}, u32[]{:S(2)}, u32[]{:S(2)}) collective-permute-start(f32[1,32,512]{2,1,0:T(8,128)S(1)} %copy.14), channel_id=1, source_target_pairs={{0,15},{1,0},{2,1},{3,2},{4,3},{5,4},{6,5},{7,6},{8,7},{9,8},{10,9... | collective-permute-start | bytes 196616 | tf_op jit(solution)/shard_map/ppermute | solution.py:12
  30.1 20.3 %collective-permute-start = (f32[1,32,512]{2,1,0:T(8,128)S(1)}, f32[1,32,512]{2,1,0:T(8,128)S(1)}, u32[]{:S(2)}, u32[]{:S(2)}) collective-permute-start(f32[1,32,512]{2,1,0:T(8,128)S(1)} %copy.12), channel_id=1, source_target_pairs={{0,1},{1,2},{2,3},{3,4},{4,5},{5,6},{6,7},{7,8},{8,9},{9,10},{10,1... | collective-permute-start | bytes 196616 | tf_op jit(solution)/shard_map/ppermute | solution.py:12
  31.2 0.8 copy-start
  33.6 1.0 copy-start.6
  56.8 12.4 %collective-permute-start.6 = (bf16[1,32,512]{2,1,0:T(8,128)(2,1)S(1)}, bf16[1,32,512]{2,1,0:T(8,128)(2,1)S(1)}, u32[]{:S(2)}, u32[]{:S(2)}) collective-permute-start(bf16[1,32,512]{2,1,0:T(8,128)(2,1)S(1)} %get-tuple-element.111), channel_id=1, source_target_pairs={{0,1},{1,2},{2,3},{3,4},{4,5},{5,6},{6,7},{7,8},{8,9},{9,10},{10,1... | collective-permute-start | bytes 98312 | tf_op jit(solution)/shard_map/ppermute | solution.py:12
  56.9 12.7 %collective-permute-start.7 = (bf16[1,32,512]{2,1,0:T(8,128)(2,1)S(1)}, bf16[1,32,512]{2,1,0:T(8,128)(2,1)S(1)}, u32[]{:S(2)}, u32[]{:S(2)}) collective-permute-start(bf16[1,32,512]{2,1,0:T(8,128)(2,1)S(1)} %get-tuple-element.112), channel_id=1, source_target_pairs={{0,15},{1,0},{2,1},{3,2},{4,3},{5,4},{6,5},{7,6},{8,7},{9,8},{10,9... | collective-permute-start | bytes 98312 | tf_op jit(solution)/shard_map/ppermute | solution.py:12
  67.1 41.5 %collective-permute-start.5 = (f32[1,32,512]{2,1,0:T(8,128)}, f32[1,32,512]{2,1,0:T(8,128)}, u32[]{:S(2)}, u32[]{:S(2)}) collective-permute-start(f32[1,32,512]{2,1,0:T(8,128)} %copy.23), channel_id=1, source_target_pairs={{0,15},{1,0},{2,1},{3,2},{4,3},{5,4},{6,5},{7,6},{8,7},{9,8},{10,9... | collective-permute-start | bytes 196616 | tf_op jit(solution)/shard_map/ppermute | solution.py:12
  68.2 39.5 %collective-permute-start.4 = (f32[1,32,512]{2,1,0:T(8,128)}, f32[1,32,512]{2,1,0:T(8,128)}, u32[]{:S(2)}, u32[]{:S(2)}) collective-permute-start(f32[1,32,512]{2,1,0:T(8,128)} %copy.21), channel_id=1, source_target_pairs={{0,1},{1,2},{2,3},{3,4},{4,5},{5,6},{6,7},{7,8},{8,9},{9,10},{10,1... | collective-permute-start | bytes 196616 | tf_op jit(solution)/shard_map/ppermute | solution.py:12
  107.6 1.8 copy-start.2
  195.1 2.3 %copy-start.5 = (f32[32,864]{1,0:T(8,128)S(1)}, f32[32,864]{1,0:T(8,128)}, u32[]{:S(2)}) copy-start(f32[32,864]{1,0:T(8,128)} %get-tuple-element.51) | copy-start | bytes 331780
  198.7 0.9 copy-start.4
Sparse Core Ops, SparseCore 0:
  105.6 89.4 all-reduce.12
where the time goes:
time: 208 us; the launch traced here: 207 us
  waiting for transfers between devices  84.8 us (41%)
  matrix products  62.4 us (30%)
  between operations  21.7 us (10%)
  starting transfers between devices  14.7 us (7%)
  local copies, waits for them, and re-layouts  12.7 us (6%)
  other arithmetic  10.7 us (5%)
    psum x1, waiting for transfers between devices, body(): first_total, second_total = lax.psum((first_grad, second_grad), 'blocks')  84.8 us
    dot_general x54, matrix products, weight_gradient(): jnp.einsum('baop,bacp->oc', cotan, moved[:, step_a:step_a + count], prefe...  26.8 us
    dot_general x81, matrix products, convolve(): jnp.einsum('oc,bacp->baop', kernel, moved[:, step_a:step_a + count], pref...  26.8 us
    ppermute x8, starting transfers between devices, shifted_2(): return lax.ppermute(value, axis, pairs)  14.7 us
    dot_general x36, matrix products, plane_adjoint(): jnp.einsum('oc,bop->bcp', kernel, piece, preferred_element_type=jnp.float32)  8.82 us
  transfers between devices with their start and end apart: 9, of which 1 were waited for; matrix products, arithmetic and copies ran while one was open for 35% of the time, Pallas kernels for 0%

commit v1 on v0

v1 whole, which is shorter than its diff:
```python
import functools

import jax
import jax.numpy as jnp
from jax import lax
from jax.experimental import pallas as pl
from jax.experimental.pallas import tpu as pltpu
from jax.sharding import PartitionSpec as P

R_CELLS = 32
CH = 32
PLANES = 8
LANES = 384
MAIN = 256
PIECES = 14
PIECE = 16
MESH = pl.DeviceIdType.MESH
POSITIONS = [0, 1, 2, 3, 4, 5, 6, 7, -2, -1, 8, 9]
F32 = jnp.float32
BF16 = jnp.bfloat16


def lane_place(position):
    index = POSITIONS.index(position)
    return index // 4, index % 4


def kernel(
    n, vertical,
    snap_ref, cot_ref, w1_ref, w2_ref, codes_ref,
    out_ref, up1_ref, up2_ref,
    halo, taps, ops1, ops2, xs, cs, hs, ps, slope, pg_nat, g1, g2, rs1, rs2, own1, own2, ag1, ag2,
    halo_send, halo_recv,
    rs1_send, rs1_recv, rs2_send, rs2_recv, ag1_send, ag1_recv, ag2_send, ag2_recv,
):
    cells = snap_ref.shape[1]
    wide = cells + 2 * vertical
    me = lax.axis_index("blocks")
    after, before = lax.rem(me + 1, n), lax.rem(me + n - 1, n)

    barrier = pltpu.get_barrier_semaphore()

    def greet(k, carry):
        pl.semaphore_signal(
            barrier, inc=1, device_id={"blocks": lax.rem(me + k, n)}, device_id_type=MESH
        )
        return carry

    lax.fori_loop(1, n, greet, 0)

    lane128 = lax.broadcasted_iota(jnp.int32, (CH, 128), 1)
    lane_block = lane128 // CH
    low, high = codes_ref[0, 0], codes_ref[0, 1]
    code_lane = jnp.where(lane_block < 2, low, high)
    flip_r = (code_lane % 2) == 1
    flip_z = (code_lane // 2) == 1

    pl.semaphore_wait(barrier, n - 1)

    copies = []
    for index, (source, rows, target, side) in enumerate([
        (snap_ref, 6 * CH, after, 0),
        (snap_ref, 0, before, 1),
        (cot_ref, 6 * CH, after, 0),
        (cot_ref, 0, before, 1),
    ]):
        copy = pltpu.make_async_remote_copy(
            src_ref=source.at[pl.ds(rows, 2 * CH)],
            dst_ref=halo.at[side, pl.ds((index // 2) * 2 * CH, 2 * CH)],
            send_sem=halo_send.at[index],
            recv_sem=halo_recv.at[index],
            device_id={"blocks": target},
            device_id_type=MESH,
        )
        copy.start()
        copies.append(copy)

    spread = (
        lax.broadcasted_iota(jnp.int32, (CH, 128), 0) == lane128 % CH
    ).astype(F32).astype(BF16)

    def build(weight_ref, ops):
        taps[...] = lax.dot_general(
            weight_ref[...], spread, (((0,), (0,)), ((), ())), preferred_element_type=F32
        )

        def tap_step(tau, carry):
            dr, dz = tau // 3, tau % 3

            def tap(da, r, z):
                start = pl.multiple_of((9 * da + 3 * r + z) * CH, CH)
                return taps[pl.ds(start, CH), :]

            plain = [tap(da, dr, dz) for da in range(3)]
            turned = [
                jnp.where(
                    flip_r,
                    jnp.where(flip_z, tap(da, 2 - dr, 2 - dz), tap(da, 2 - dr, dz)),
                    jnp.where(flip_z, tap(da, dr, 2 - dz), plain[da]),
                )
                for da in range(3)
            ]
            for x, position in enumerate(POSITIONS):
                for tile in range(3):
                    value = jnp.zeros((CH, 128), F32)
                    for da in range(3):
                        wanted = position - da + 1
                        if wanted < -2 or wanted > 9:
                            continue
                        place = lane_place(wanted)
                        if place[0] != tile:
                            continue
                        source = turned[da] if tile == 2 else plain[da]
                        value = jnp.where(lane_block == place[1], source, value)
                    ops[tau, pl.ds(x * CH, CH), pl.ds(tile * 128, 128)] = value.astype(BF16)
            return carry

        lax.fori_loop(0, 9, tap_step, 0)

    def put(dst, start, first_lane, value):
        rows, lanes = value.shape
        z = lax.broadcasted_iota(jnp.int32, (rows, lanes), 0) % vertical
        moved = [
            jnp.where(z == 0, 0.0, pltpu.roll(value, 1, 0)),
            value,
            jnp.where(z == vertical - 1, 0.0, pltpu.roll(value, rows - 1, 0)),
        ]
        for dz in range(3):
            dst[dz, pl.ds(start, rows), pl.ds(first_lane, lanes)] = moved[dz].astype(BF16)

    edge = jnp.zeros((3, vertical, LANES), BF16)
    for field in (xs, cs, hs, ps):
        field[:, pl.ds(0, vertical), :] = edge
        field[:, pl.ds(wide - vertical, vertical), :] = edge

    put(xs, vertical, 0, snap_ref[...].astype(F32).T)
    put(cs, vertical, 0, cot_ref[...].astype(F32).T)
    build(w1_ref, ops1)
    build(w2_ref, ops2)

    row_cell = lax.broadcasted_iota(jnp.int32, (cells, cells), 0)
    column_cell = lax.broadcasted_iota(jnp.int32, (cells, cells), 1)
    radial_bits = cells - vertical
    swaps = []
    for code in (low, high):
        mask = (code % 2) * radial_bits + (code // 2) * (vertical - 1)
        swaps.append((row_cell == jnp.bitwise_xor(column_cell, mask)).astype(F32).astype(BF16))

    for copy in copies:
        copy.wait()

    sides = [
        jnp.dot(halo[side], swaps[side], preferred_element_type=F32) for side in range(2)
    ]
    put(xs, vertical, MAIN, jnp.concatenate([sides[0][: 2 * CH], sides[1][: 2 * CH]], axis=0).T)
    put(cs, vertical, MAIN, jnp.concatenate([sides[0][2 * CH :], sides[1][2 * CH :]], axis=0).T)

    chunk = 256

    def forward(field, ops, start):
        total = None
        for dr in range(3):
            for dz in range(3):
                term = jnp.dot(
                    field[dz, pl.ds(start + dr * vertical, chunk), :],
                    ops[3 * dr + dz],
                    preferred_element_type=F32,
                )
                total = term if total is None else total + term
        return total

    def backward(field, ops, start, outs):
        total = None
        for dr in range(3):
            for dz in range(3):
                term = lax.dot_general(
                    field[2 - dz, pl.ds(start + (2 - dr) * vertical, chunk), :],
                    ops[3 * dr + dz, pl.ds(0, outs), :],
                    (((1,), (1,)), ((), ())),
                    preferred_element_type=F32,
                )
                total = term if total is None else total + term
        return total

    def gradient(left, field, result):
        lane = lax.broadcasted_iota(jnp.int32, (CH, 128), 1) // CH
        found = {}
        for dr in range(3):
            for dz in range(3):
                full = jnp.dot(
                    left[...],
                    field[dz, pl.ds(dr * vertical, cells), :],
                    preferred_element_type=F32,
                )
                for da in range(3):
                    total = None
                    for a in range(PLANES):
                        tile, block = lane_place(a + da - 1)
                        piece = full[a * CH : (a + 1) * CH, tile * 128 : (tile + 1) * 128]
                        term = jnp.where(lane == block, piece, 0.0)
                        total = term if total is None else total + term
                    total = total + pltpu.roll(total, 64, 1)
                    total = total + pltpu.roll(total, 32, 1)
                    found[9 * da + 3 * dr + dz] = total
        for tile in range(7):
            value = jnp.zeros((CH, 128), F32)
            for block in range(4):
                if 4 * tile + block < 27:
                    value = jnp.where(lane == block, found[4 * tile + block], value)
            result[pl.ds(tile * CH, CH), :] = value

    def scatter_copy(grad, slots, send, recv, owner, source):
        return pltpu.make_async_remote_copy(
            src_ref=grad.at[pl.ds(pl.multiple_of(owner * PIECE, PIECE), PIECE)],
            dst_ref=slots.at[source],
            send_sem=send.at[owner],
            recv_sem=recv.at[source],
            device_id={"blocks": owner},
            device_id_type=MESH,
        )

    def scatter_start(grad, slots, send, recv):
        def one(k, carry):
            owner = lax.rem(me + k, n)

            @pl.when(owner < PIECES)
            def _():
                scatter_copy(grad, slots, send, recv, owner, me).start()

            return carry

        lax.fori_loop(1, n, one, 0)

        @pl.when(me < PIECES)
        def _():
            slots[me] = grad[pl.ds(pl.multiple_of(me * PIECE, PIECE), PIECE), :]

    def gather_copy(own, gathered, send, recv, owner, target):
        return pltpu.make_async_remote_copy(
            src_ref=own,
            dst_ref=gathered.at[owner],
            send_sem=send.at[target],
            recv_sem=recv.at[owner],
            device_id={"blocks": target},
            device_id_type=MESH,
        )

    def reduce_and_gather(grad, slots, send, recv, own, gathered, gsend, grecv):
        @pl.when(me < PIECES)
        def _():
            def one(k, carry):
                source = lax.rem(me + k, n)
                scatter_copy(grad, slots, send, recv, me, source).wait_recv()
                return carry

            lax.fori_loop(1, n, one, 0)
            total = jnp.sum(slots[...], axis=0).astype(BF16)
            own[...] = total
            gathered[me] = total

            def out(k, carry):
                gather_copy(own, gathered, gsend, grecv, me, lax.rem(me + k, n)).start()
                return carry

            lax.fori_loop(1, n, out, 0)

    def finish(grad, slots, send, recv, own, gathered, gsend, grecv, up_ref):
        def sent(k, carry):
            owner = lax.rem(me + k, n)

            @pl.when(owner < PIECES)
            def _():
                scatter_copy(grad, slots, send, recv, owner, me).wait_send()
                gather_copy(own, gathered, gsend, grecv, owner, me).wait_recv()

            return carry

        lax.fori_loop(1, n, sent, 0)
        value = gathered[...].astype(F32).reshape(PIECES * PIECE, 128)
        scale = lax.rsqrt(jnp.sum(value * value) / (CH * 27 * CH) + 1e-06)
        value = value * scale
        for tile in range(7):
            lanes = 128 if tile < 6 else 96
            up_ref[:, pl.ds(tile * 128, lanes)] = value[tile * CH : (tile + 1) * CH, :lanes]

        @pl.when(me < PIECES)
        def _():
            def out(k, carry):
                gather_copy(own, gathered, gsend, grecv, me, lax.rem(me + k, n)).wait_send()
                return carry

            lax.fori_loop(1, n, out, 0)

    set1 = (g1, rs1, rs1_send, rs1_recv, own1, ag1, ag1_send, ag1_recv)
    set2 = (g2, rs2, rs2_send, rs2_recv, own2, ag2, ag2_send, ag2_recv)

    for start in range(0, cells, chunk):
        pre = forward(xs, ops1, start)
        s = 1.0 / (1.0 + jnp.exp(-pre))
        hidden = (pre * s).astype(BF16)
        slope[pl.ds(start, chunk), :] = s * (1.0 + pre * (1.0 - s))
        put(hs, start + vertical, 0, hidden.astype(F32))

    gradient(cot_ref, hs, g2)
    scatter_start(*set2[:4])

    for start in range(0, cells, chunk):
        back = backward(cs, ops2, start, LANES)
        value = (back * slope[pl.ds(start, chunk), :]).astype(BF16).astype(F32)
        put(ps, start + vertical, 0, value)
        pg_nat[:, pl.ds(start, chunk)] = value[:, :MAIN].T.astype(BF16)

    gradient(pg_nat, xs, g1)
    scatter_start(*set1[:4])
    reduce_and_gather(*set2)

    for start in range(0, cells, chunk):
        back = backward(ps, ops1, start, MAIN)
        out_ref[:, pl.ds(start, chunk)] = back.T + cot_ref[:, pl.ds(start, chunk)].astype(F32)

    reduce_and_gather(*set1)
    finish(*set2, up2_ref)
    finish(*set1, up1_ref)


def solution(mesh):
    n = mesh.shape["blocks"]

    def body(snapshot, cotangent, first_weight, second_weight, face_codes):
        cells = snapshot.shape[3]
        vertical = cells // R_CELLS
        wide = cells + 2 * vertical
        flat = (PLANES * CH, cells)
        vmem = pl.BlockSpec(memory_space=pltpu.VMEM)
        dma = pltpu.SemaphoreType.DMA
        grad, up1, up2 = pl.pallas_call(
            functools.partial(kernel, n, vertical),
            out_shape=(
                jax.ShapeDtypeStruct(flat, F32),
                jax.ShapeDtypeStruct(first_weight.shape, F32),
                jax.ShapeDtypeStruct(second_weight.shape, F32),
            ),
            in_specs=[vmem] * 4 + [pl.BlockSpec(memory_space=pltpu.SMEM)],
            out_specs=(vmem, vmem, vmem),
            scratch_shapes=[
                pltpu.VMEM((2, 4 * CH, cells), BF16),
                pltpu.VMEM((27 * CH, 128), F32),
                pltpu.VMEM((9, LANES, LANES), BF16),
                pltpu.VMEM((9, LANES, LANES), BF16),
                pltpu.VMEM((3, wide, LANES), BF16),
                pltpu.VMEM((3, wide, LANES), BF16),
                pltpu.VMEM((3, wide, LANES), BF16),
                pltpu.VMEM((3, wide, LANES), BF16),
                pltpu.VMEM((cells, LANES), F32),
                pltpu.VMEM(flat, BF16),
                pltpu.VMEM((PIECES * PIECE, 128), F32),
                pltpu.VMEM((PIECES * PIECE, 128), F32),
                pltpu.VMEM((n, PIECE, 128), F32),
                pltpu.VMEM((n, PIECE, 128), F32),
                pltpu.VMEM((PIECE, 128), BF16),
                pltpu.VMEM((PIECE, 128), BF16),
                pltpu.VMEM((PIECES, PIECE, 128), BF16),
                pltpu.VMEM((PIECES, PIECE, 128), BF16),
                dma((4,)),
                dma((4,)),
                dma((PIECES,)),
                dma((n,)),
                dma((PIECES,)),
                dma((n,)),
                dma((n,)),
                dma((PIECES,)),
                dma((n,)),
                dma((PIECES,)),
            ],
            compiler_params=pltpu.CompilerParams(
                collective_id=0, has_side_effects=True, vmem_limit_bytes=48 * 1024 * 1024
            ),
        )(
            snapshot.reshape(flat),
            cotangent.reshape(flat),
            first_weight,
            second_weight,
            face_codes,
        )
        return grad.reshape(snapshot.shape), up1, up2

    return jax.shard_map(
        body,
        mesh=mesh,
        in_specs=(
            P("groups", "blocks", None, None),
            P("groups", "blocks", None, None),
            P(),
            P(),
            P(("groups", "blocks"), None),
        ),
        out_specs=(P("groups", "blocks", None, None), P("groups", None), P("groups", None)),
        check_vma=False,
    )
```

time: 208 us -> 37.7 us (0.18)
  waiting for transfers between devices: 84.8 us -> 0 us
  matrix products: 62.4 us -> 0 us
  Pallas kernels: 0 us -> 30.5 us
  between operations: 21.7 us -> 0.65 us
  starting transfers between devices: 14.7 us -> 0 us
  other arithmetic: 10.7 us -> 0 us
  local copies, waits for them, and re-layouts: 12.7 us -> 6.27 us
    psum x1 -> x0, waiting for transfers between devices: 84.8 us -> none  [body(): first_total, second_total = lax.psum((first_grad, second_grad), 'blocks')]
    dot_general x171 -> x0, matrix products: 62.4 us -> none  [the longest x54 26.8 us: weight_gradient(): jnp.einsum('baop,bacp->oc', cotan, moved[:, step_a:step_a + count], prefe...]
    pallas_call x0 -> x1, Pallas kernels: none -> 30.5 us  [body(): pl.pallas_call(functools.partial(kernel, n, vertical), out_shape=(jax.Sha...]
    ppermute x8 -> x0, starting transfers between devices: 14.7 us -> none  [shifted_2(): return lax.ppermute(value, axis, pairs)]
    select_n x20 -> x0, other arithmetic: 4.5 us -> none  [the longest x4 3.91 us: shifted(): return jnp.where(valid, piece, jnp.zeros((), field.dtype))]
    unnamed x18 -> x13, local copies, waits for them, and re-layouts: 3.25 us -> 6.27 us
    reshape x8 -> x0, local copies, waits for them, and re-layouts: 2.57 us -> none  [the longest x4 1.66 us: flip_plane(): return grid.reshape(batch_count, channels, radial * vertical)]
    concatenate x2 -> x0, local copies, waits for them, and re-layouts: 2.55 us -> none  [weight_gradient(): return jnp.concatenate([found[index] for index in range(27)], axis=1)]
  transfers between devices with their start and end apart: 9 -> 0, of which waited for: 1 -> 0; matrix products, arithmetic and copies ran while one was open for 35% -> 0% of each run, Pallas kernels for 0% -> 0%
where the time goes in v1:
time: 37.7 us; the launch traced here: 37.4 us
  Pallas kernels  30.5 us (81%)
  local copies, waits for them, and re-layouts  6.27 us (17%)
  between operations  0.65 us (2%)
    pallas_call x1, Pallas kernels, body(): pl.pallas_call(functools.partial(kernel, n, vertical), out_shape=(jax.Sha...  30.5 us
    unnamed x13, local copies, waits for them, and re-layouts  6.27 us

profile of v1, /device:TPU:0, one launch (start us, length us, event | category | flops | bytes accessed | tf_op | source)
XLA Modules:
  0.0 37.4 jit_solution(8768901734616200258)
XLA Ops:
  0.6 0.0 copy-start.4
  0.6 0.6 %copy-done.4 = s32[1,2]{1,0:T(1,128)S(1)} copy-done((s32[1,2]{1,0:T(1,128)S(1)}, s32[1,2]{1,0:T(1,128)}, u32[]{:S(2)}) %copy-start.4) | copy-done | bytes 32
  1.3 0.0 copy-start
  1.3 0.9 %copy-done = bf16[1,8,32,512]{3,2,1,0:T(8,128)(2,1)S(1)} copy-done((bf16[1,8,32,512]{3,2,1,0:T(8,128)(2,1)S(1)}, bf16[1,8,32,512]{3,2,1,0:T(8,128)(2,1)}, u32[]{:S(2)}) %copy-start) | copy-done | bytes 262168
  2.2 0.0 copy-start.1
  2.2 0.9 %copy-done.1 = bf16[1,8,32,512]{3,2,1,0:T(8,128)(2,1)S(1)} copy-done((bf16[1,8,32,512]{3,2,1,0:T(8,128)(2,1)S(1)}, bf16[1,8,32,512]{3,2,1,0:T(8,128)(2,1)}, u32[]{:S(2)}) %copy-start.1) | copy-done | bytes 262168
  3.2 0.0 copy-start.2
  3.2 0.8 %copy-done.2 = bf16[32,864]{1,0:T(8,128)(2,1)S(1)} copy-done((bf16[32,864]{1,0:T(8,128)(2,1)S(1)}, bf16[32,864]{1,0:T(8,128)(2,1)}, u32[]{:S(2)}) %copy-start.2) | copy-done | bytes 55320
  4.0 0.0 copy-start.3
  4.0 0.8 %copy-done.3 = bf16[32,864]{1,0:T(8,128)(2,1)S(1)} copy-done((bf16[32,864]{1,0:T(8,128)(2,1)S(1)}, bf16[32,864]{1,0:T(8,128)(2,1)}, u32[]{:S(2)}) %copy-start.3) | copy-done | bytes 55320
  4.8 30.5 %shard_map.76 = (f32[256,512]{1,0:T(8,128)S(1)}, f32[32,864]{1,0:T(8,128)S(1)}, f32[32,864]{1,0:T(8,128)S(1)}) custom-call(bf16[256,512]{1,0:T(8,128)(2,1)S(1)} %bitcast.4, bf16[256,512]{1,0:T(8,128)(2,1)S(1)} %bitcast.5, bf16[32,864]{1,0:T(8,128)(2,1)S(1)} %copy-done.2, bf16[32,864]{1,0:T(8,128)(2,1)S(1)} %copy-done.3, s32[1,2]{1,0:T(1,128)S(1)} %copy-done.4), custom_call_target="tpu_custom_call" | custom-call | tf_op jit(solution)/shard_map/pallas_call | solution.py:336
  35.3 0.8 %copy.11 = f32[1,8,32,512]{3,2,1,0:T(8,128)} copy(f32[1,8,32,512]{3,2,1,0:T(8,128)S(1)} %bitcast.3) | data formatting | bytes 1048576
  36.1 0.6 %copy.12 = f32[32,864]{1,0:T(8,128)} copy(f32[32,864]{1,0:T(8,128)S(1)} %get-tuple-element.13) | data formatting | bytes 221184
  36.8 0.6 %copy.13 = f32[32,864]{1,0:T(8,128)} copy(f32[32,864]{1,0:T(8,128)S(1)} %get-tuple-element.14) | data formatting | bytes 221184
Async XLA Ops:
  0.6 0.7 %copy-start.4 = (s32[1,2]{1,0:T(1,128)S(1)}, s32[1,2]{1,0:T(1,128)}, u32[]{:S(2)}) copy-start(s32[1,2]{1,0:T(1,128)} %codes_ref.1) | copy-start | bytes 28
  1.3 0.9 %copy-start = (bf16[1,8,32,512]{3,2,1,0:T(8,128)(2,1)S(1)}, bf16[1,8,32,512]{3,2,1,0:T(8,128)(2,1)}, u32[]{:S(2)}) copy-start(bf16[1,8,32,512]{3,2,1,0:T(8,128)(2,1)} %param.5) | copy-start | bytes 786436
  2.2 0.9 %copy-start.1 = (bf16[1,8,32,512]{3,2,1,0:T(8,128)(2,1)S(1)}, bf16[1,8,32,512]{3,2,1,0:T(8,128)(2,1)}, u32[]{:S(2)}) copy-start(bf16[1,8,32,512]{3,2,1,0:T(8,128)(2,1)} %param.6) | copy-start | bytes 786436
  3.2 0.8 %copy-start.2 = (bf16[32,864]{1,0:T(8,128)(2,1)S(1)}, bf16[32,864]{1,0:T(8,128)(2,1)}, u32[]{:S(2)}) copy-start(bf16[32,864]{1,0:T(8,128)(2,1)} %w1_ref.1) | copy-start | bytes 165892
  4.0 0.8 %copy-start.3 = (bf16[32,864]{1,0:T(8,128)(2,1)S(1)}, bf16[32,864]{1,0:T(8,128)(2,1)}, u32[]{:S(2)}) copy-start(bf16[32,864]{1,0:T(8,128)(2,1)} %w2_ref.1) | copy-start | bytes 165892

commit v2 on v1

v2 whole, which is shorter than its diff:
```python
import functools

import jax
import jax.numpy as jnp
from jax import lax
from jax.experimental import pallas as pl
from jax.experimental.pallas import tpu as pltpu
from jax.sharding import PartitionSpec as P

R_CELLS = 32
CH = 32
PLANES = 8
LANES = 384
MAIN = 256
PIECES = 14
PIECE = 16
MESH = pl.DeviceIdType.MESH
POSITIONS = [0, 1, 2, 3, 4, 5, 6, 7, -2, -1, 8, 9]
F32 = jnp.float32
BF16 = jnp.bfloat16


def lane_place(position):
    index = POSITIONS.index(position)
    return index // 4, index % 4


HALO = [-2, -1, 8, 9]
INNER = list(range(PLANES))


def kernel(
    n, vertical,
    snap_in, cot_in, w1_in, w2_in, codes_in,
    out_ref, up1_ref, up2_ref,
    snap_ref, cot_ref, w1_ref, w2_ref, codes_ref,
    halo, taps, main1, main2, side1, side2, back1, edge1, edge2,
    xs, xh, xe, cs, ch, ce, hs, hh, ps, ph,
    pg_nat, cot_edge, g1, g2, rs1, rs2, own1, own2, ag1, ag2,
    load_sem, halo_send, halo_recv,
    rs1_send, rs1_recv, rs2_send, rs2_recv, ag1_send, ag1_recv, ag2_send, ag2_recv,
):
    cells = snap_ref.shape[1]
    wide = cells + 2 * vertical
    me = lax.axis_index("blocks")
    after, before = lax.rem(me + 1, n), lax.rem(me + n - 1, n)

    barrier = pltpu.get_barrier_semaphore()

    def greet(k, carry):
        pl.semaphore_signal(
            barrier, inc=1, device_id={"blocks": lax.rem(me + k, n)}, device_id_type=MESH
        )
        return carry

    lax.fori_loop(1, n, greet, 0)

    loads = [
        pltpu.make_async_copy(source, target, load_sem.at[index])
        for index, (source, target) in enumerate([
            (codes_in, codes_ref), (w1_in, w1_ref), (w2_in, w2_ref), (snap_in, snap_ref), (cot_in, cot_ref)
        ])
    ]
    for load in loads:
        load.start()

    for field in (xs, cs, hs, ps):
        field[:, pl.ds(0, vertical), :] = jnp.zeros((3, vertical, MAIN), BF16)
        field[:, pl.ds(wide - vertical, vertical), :] = jnp.zeros((3, vertical, MAIN), BF16)
    for field in (xh, ch, hh, ph, xe, ce):
        field[pl.ds(0, vertical), :] = jnp.zeros((vertical, field.shape[1]), BF16)
        field[pl.ds(wide - vertical, vertical), :] = jnp.zeros((vertical, field.shape[1]), BF16)

    pl.semaphore_wait(barrier, n - 1)

    copies = []
    for index, (source, rows, target, side) in enumerate([
        (snap_in, 6 * CH, after, 0),
        (snap_in, 0, before, 1),
        (cot_in, 6 * CH, after, 0),
        (cot_in, 0, before, 1),
    ]):
        copy = pltpu.make_async_remote_copy(
            src_ref=source.at[pl.ds(rows, 2 * CH)],
            dst_ref=halo.at[side, pl.ds((index // 2) * 2 * CH, 2 * CH)],
            send_sem=halo_send.at[index],
            recv_sem=halo_recv.at[index],
            device_id={"blocks": target},
            device_id_type=MESH,
        )
        copy.start()
        copies.append(copy)

    for load in loads:
        load.wait()

    lane_block = lax.broadcasted_iota(jnp.int32, (CH, 128), 1) // CH
    low, high = codes_ref[0, 0], codes_ref[0, 1]
    code_lane = jnp.where(lane_block < 2, low, high)
    flip_r = (code_lane % 2) == 1
    flip_z = (code_lane // 2) == 1
    spread = (
        lax.broadcasted_iota(jnp.int32, (CH, 128), 0)
        == lax.broadcasted_iota(jnp.int32, (CH, 128), 1) % CH
    ).astype(F32).astype(BF16)

    def tap(da, r, z):
        start = pl.multiple_of((9 * da + 3 * r + z) * CH, CH)
        return taps[pl.ds(start, CH), :]

    def turned(da, r, z):
        return jnp.where(
            flip_r,
            jnp.where(flip_z, tap(da, 2 - r, 2 - z), tap(da, 2 - r, z)),
            jnp.where(flip_z, tap(da, r, 2 - z), tap(da, r, z)),
        )

    def block(x, columns, dr):
        value = jnp.zeros((CH, 128), F32)
        for index, column in enumerate(columns):
            if column is None:
                continue
            y, dz = column
            da = x - y + 1
            if 0 <= da <= 2:
                source = turned(da, dr, dz) if y in HALO else tap(da, dr, dz)
                value = jnp.where(lane_block == index, source, value)
        return value.astype(BF16)

    def plane_tiles(dz):
        return [[(y, dz) for y in group] for group in (INNER[:4], INNER[4:], HALO)]

    def spread_taps(weight_ref):
        taps[...] = lax.dot_general(
            weight_ref[...], spread, (((0,), (0,)), ((), ())), preferred_element_type=F32
        )

    def fill(ref, lead, row, tile, value):
        ref[lead, pl.ds(row * CH, CH), pl.ds(tile * 128, 128)] = value

    def build_main(dr, main):
        for dz in range(3):
            for row, x in enumerate(INNER):
                for tile in range(2):
                    fill(main, 3 * dr + dz, row, tile, block(x, plane_tiles(dz)[tile], dr))

    def build_forward(dr, side, edge):
        row = 0
        for dz in range(3):
            for x in HALO:
                for tile in range(3):
                    fill(side, dr, row, tile, block(x, plane_tiles(dz)[tile], dr))
                row += 1
        row = 0
        for dz in range(3):
            for x in (0, 7):
                fill(edge, dr, row, 0, block(x, plane_tiles(dz)[2], dr))
                row += 1
        for row in (6, 7):
            fill(edge, dr, row, 0, jnp.zeros((CH, 128), BF16))

    def build_backward(dr, side, edge, planes):
        for row, x in enumerate(planes):
            for moved in range(3):
                fill(side, dr, row, moved, block(x, plane_tiles(2 - moved)[2], dr))
        if edge is not None:
            for row, x in enumerate(HALO):
                fill(edge, dr, row, 0, block(x, [(0, 2), (7, 2), (0, 1), (7, 1)], dr))
                fill(edge, dr, row, 1, block(x, [(0, 0), (7, 0), None, None], dr))

    def shifts(value):
        rows, lanes = value.shape
        z = lax.broadcasted_iota(jnp.int32, (rows, lanes), 0) % vertical
        return [
            jnp.where(z == 0, 0.0, pltpu.roll(value, 1, 0)),
            value,
            jnp.where(z == vertical - 1, 0.0, pltpu.roll(value, rows - 1, 0)),
        ]

    inside = pl.ds(vertical, cells)

    def put_main(dst, value):
        for dz, moved in enumerate(shifts(value)):
            dst[dz, inside, :] = moved.astype(BF16)

    def put_halo(dst, value):
        for dz, moved in enumerate(shifts(value)):
            dst[inside, pl.ds(dz * 128, 128)] = moved.astype(BF16)

    def put_edge(dst, source):
        ends = jnp.concatenate([source[:CH, :], source[7 * CH :, :]] * 2, axis=0)
        moved = shifts(ends.astype(F32).T)
        first = lax.broadcasted_iota(jnp.int32, (cells, 128), 1) < 64
        dst[inside, pl.ds(0, 128)] = jnp.where(first, moved[0], moved[1]).astype(BF16)
        dst[inside, pl.ds(128, 128)] = jnp.where(first, moved[2], 0.0).astype(BF16)

    put_main(xs, snap_ref[...].astype(F32).T)
    put_edge(xe, snap_ref)
    spread_taps(w1_ref)

    def build1(dr, carry):
        build_main(dr, main1)
        build_forward(dr, side1, edge1)
        build_backward(dr, back1, None, INNER)
        return carry

    lax.fori_loop(0, 3, build1, 0)
    put_main(cs, cot_ref[...].astype(F32).T)
    put_edge(ce, cot_ref)
    cot_edge[pl.ds(0, CH), :] = cot_ref[pl.ds(0, CH), :]
    cot_edge[pl.ds(CH, CH), :] = cot_ref[pl.ds(7 * CH, CH), :]
    spread_taps(w2_ref)

    def build2(dr, carry):
        build_main(dr, main2)
        build_backward(dr, side2, edge2, INNER + HALO)
        return carry

    lax.fori_loop(0, 3, build2, 0)

    row_cell = lax.broadcasted_iota(jnp.int32, (cells, cells), 0)
    column_cell = lax.broadcasted_iota(jnp.int32, (cells, cells), 1)
    radial_bits = cells - vertical
    swaps = []
    for code in (low, high):
        mask = (code % 2) * radial_bits + (code // 2) * (vertical - 1)
        swaps.append((row_cell == jnp.bitwise_xor(column_cell, mask)).astype(F32).astype(BF16))

    for copy in copies:
        copy.wait()

    sides = [
        jnp.dot(halo[side], swaps[side], preferred_element_type=F32) for side in range(2)
    ]
    put_halo(xh, jnp.concatenate([sides[0][: 2 * CH], sides[1][: 2 * CH]], axis=0).T)
    put_halo(ch, jnp.concatenate([sides[0][2 * CH :], sides[1][2 * CH :]], axis=0).T)

    def added(total, term):
        return term if total is None else total + term

    def nn(left, right):
        return jnp.dot(left, right, preferred_element_type=F32)

    def nt(left, right):
        return lax.dot_general(left, right, (((1,), (1,)), ((), ())), preferred_element_type=F32)

    def up(step_r):
        return pl.ds(step_r * vertical, cells)

    def forward():
        inner, outer = None, None
        for dr in range(3):
            for dz in range(3):
                inner = added(inner, nn(xs[dz, up(dr), :], main1[3 * dr + dz]))
            inner = added(inner, nn(xh[up(dr), :], side1[dr, :, :MAIN]))
            outer = added(outer, nn(xh[up(dr), :], side1[dr, :, MAIN:]))
            outer = added(outer, nn(xe[up(dr), :], edge1[dr]))
        return inner, outer

    def backward(field, halos, main, side):
        inner = None
        for dr in range(3):
            for dz in range(3):
                inner = added(inner, nt(field[2 - dz, up(2 - dr), :], main[3 * dr + dz]))
            inner = added(inner, nt(halos[up(2 - dr), :], side[dr, :MAIN, :]))
        return inner

    def backward_outer(halos, ends, side, edge):
        outer = None
        for dr in range(3):
            outer = added(outer, nt(halos[up(2 - dr), :], side[dr, MAIN:, :]))
            outer = added(outer, nt(ends[up(2 - dr), :], edge[dr]))
        return outer

    def gradient(left, ends, field, halos, result):
        found = {}
        for dr in range(3):
            outer = nn(ends, halos[up(dr), :])
            for dz in range(3):
                full = nn(left, field[dz, up(dr), :])
                for da in range(3):
                    total = None
                    for a in range(PLANES):
                        tile, place = lane_place(a + da - 1)
                        if tile == 2:
                            row = 0 if a == 0 else CH
                            piece = outer[row : row + CH, dz * 128 : (dz + 1) * 128]
                        else:
                            piece = full[a * CH : (a + 1) * CH, tile * 128 : (tile + 1) * 128]
                        total = added(total, jnp.where(lane_block == place, piece, 0.0))
                    total = total + pltpu.roll(total, 64, 1)
                    total = total + pltpu.roll(total, 32, 1)
                    found[9 * da + 3 * dr + dz] = total
        for tile in range(7):
            value = jnp.zeros((CH, 128), F32)
            for place in range(4):
                if 4 * tile + place < 27:
                    value = jnp.where(lane_block == place, found[4 * tile + place], value)
            result[pl.ds(tile * CH, CH), :] = value

    def scatter_copy(grad, slots, send, recv, owner, source):
        return pltpu.make_async_remote_copy(
            src_ref=grad.at[pl.ds(pl.multiple_of(owner * PIECE, PIECE), PIECE)],
            dst_ref=slots.at[source],
            send_sem=send.at[owner],
            recv_sem=recv.at[source],
            device_id={"blocks": owner},
            device_id_type=MESH,
        )

    def scatter_start(grad, slots, send, recv):
        def one(k, carry):
            owner = lax.rem(me + k, n)

            @pl.when(owner < PIECES)
            def _():
                scatter_copy(grad, slots, send, recv, owner, me).start()

            return carry

        lax.fori_loop(1, n, one, 0)

        @pl.when(me < PIECES)
        def _():
            slots[me] = grad[pl.ds(pl.multiple_of(me * PIECE, PIECE), PIECE), :]

    def gather_copy(own, gathered, send, recv, owner, target):
        return pltpu.make_async_remote_copy(
            src_ref=own,
            dst_ref=gathered.at[owner],
            send_sem=send.at[target],
            recv_sem=recv.at[owner],
            device_id={"blocks": target},
            device_id_type=MESH,
        )

    def reduce_and_gather(grad, slots, send, recv, own, gathered, gsend, grecv):
        @pl.when(me < PIECES)
        def _():
            def one(k, carry):
                source = lax.rem(me + k, n)
                scatter_copy(grad, slots, send, recv, me, source).wait_recv()
                return carry

            lax.fori_loop(1, n, one, 0)
            total = jnp.sum(slots[...], axis=0).astype(BF16)
            own[...] = total
            gathered[me] = total

            def out(k, carry):
                gather_copy(own, gathered, gsend, grecv, me, lax.rem(me + k, n)).start()
                return carry

            lax.fori_loop(1, n, out, 0)

    def finish(grad, slots, send, recv, own, gathered, gsend, grecv, up_ref):
        def sent(k, carry):
            owner = lax.rem(me + k, n)

            @pl.when(owner < PIECES)
            def _():
                scatter_copy(grad, slots, send, recv, owner, me).wait_send()
                gather_copy(own, gathered, gsend, grecv, owner, me).wait_recv()

            return carry

        lax.fori_loop(1, n, sent, 0)
        value = gathered[...].astype(F32).reshape(PIECES * PIECE, 128)
        scale = lax.rsqrt(jnp.sum(value * value) / (CH * 27 * CH) + 1e-06)
        value = value * scale
        for tile in range(7):
            lanes = 128 if tile < 6 else 96
            up_ref[:, pl.ds(tile * 128, lanes)] = value[tile * CH : (tile + 1) * CH, :lanes]

        @pl.when(me < PIECES)
        def _():
            def out(k, carry):
                gather_copy(own, gathered, gsend, grecv, me, lax.rem(me + k, n)).wait_send()
                return carry

            lax.fori_loop(1, n, out, 0)

    set1 = (g1, rs1, rs1_send, rs1_recv, own1, ag1, ag1_send, ag1_recv)
    set2 = (g2, rs2, rs2_send, rs2_recv, own2, ag2, ag2_send, ag2_recv)

    def activate(pre):
        s = 1.0 / (1.0 + jnp.exp(-pre))
        return (pre * s).astype(BF16).astype(F32), s * (1.0 + pre * (1.0 - s))

    inner, outer = forward()
    hidden, slope = activate(inner)
    hidden_outer, slope_outer = activate(outer)
    put_main(hs, hidden)
    put_halo(hh, hidden_outer)

    gradient(cot_ref[...], cot_edge[...], hs, hh, g2)
    scatter_start(*set2[:4])

    value = (backward(cs, ch, main2, side2) * slope).astype(BF16).astype(F32)
    put_main(ps, value)
    pg_nat[...] = value.T.astype(BF16)
    value = (backward_outer(ch, ce, side2, edge2) * slope_outer).astype(BF16).astype(F32)
    put_halo(ph, value)

    ends = jnp.concatenate([pg_nat[:CH, :], pg_nat[7 * CH :, :]], axis=0)
    gradient(pg_nat[...], ends, xs, xh, g1)
    scatter_start(*set1[:4])
    reduce_and_gather(*set2)

    out_ref[...] = backward(ps, ph, main1, back1).T + cot_ref[...].astype(F32)

    reduce_and_gather(*set1)
    finish(*set2, up2_ref)
    finish(*set1, up1_ref)


def solution(mesh):
    n = mesh.shape["blocks"]

    def body(snapshot, cotangent, first_weight, second_weight, face_codes):
        cells = snapshot.shape[3]
        vertical = cells // R_CELLS
        wide = cells + 2 * vertical
        flat = (PLANES * CH, cells)
        vmem = pl.BlockSpec(memory_space=pltpu.VMEM)
        dma = pltpu.SemaphoreType.DMA
        grad, up1, up2 = pl.pallas_call(
            functools.partial(kernel, n, vertical),
            out_shape=(
                jax.ShapeDtypeStruct(flat, F32),
                jax.ShapeDtypeStruct(first_weight.shape, F32),
                jax.ShapeDtypeStruct(second_weight.shape, F32),
            ),
            in_specs=[pl.BlockSpec(memory_space=pltpu.HBM)] * 5,
            out_specs=(vmem, vmem, vmem),
            scratch_shapes=[
                pltpu.VMEM(flat, BF16),
                pltpu.VMEM(flat, BF16),
                pltpu.VMEM(first_weight.shape, BF16),
                pltpu.VMEM(second_weight.shape, BF16),
                pltpu.SMEM((1, 2), jnp.int32),
                pltpu.VMEM((2, 4 * CH, cells), BF16),
                pltpu.VMEM((27 * CH, 128), F32),
                pltpu.VMEM((9, MAIN, MAIN), BF16),
                pltpu.VMEM((9, MAIN, MAIN), BF16),
                pltpu.VMEM((3, LANES, LANES), BF16),
                pltpu.VMEM((3, LANES, LANES), BF16),
                pltpu.VMEM((3, MAIN, LANES), BF16),
                pltpu.VMEM((3, MAIN, 128), BF16),
                pltpu.VMEM((3, 128, MAIN), BF16),
                pltpu.VMEM((3, wide, MAIN), BF16),
                pltpu.VMEM((wide, LANES), BF16),
                pltpu.VMEM((wide, MAIN), BF16),
                pltpu.VMEM((3, wide, MAIN), BF16),
                pltpu.VMEM((wide, LANES), BF16),
                pltpu.VMEM((wide, MAIN), BF16),
                pltpu.VMEM((3, wide, MAIN), BF16),
                pltpu.VMEM((wide, LANES), BF16),
                pltpu.VMEM((3, wide, MAIN), BF16),
                pltpu.VMEM((wide, LANES), BF16),
                pltpu.VMEM(flat, BF16),
                pltpu.VMEM((2 * CH, cells), BF16),
                pltpu.VMEM((PIECES * PIECE, 128), F32),
                pltpu.VMEM((PIECES * PIECE, 128), F32),
                pltpu.VMEM((n, PIECE, 128), F32),
                pltpu.VMEM((n, PIECE, 128), F32),
                pltpu.VMEM((PIECE, 128), BF16),
                pltpu.VMEM((PIECE, 128), BF16),
                pltpu.VMEM((PIECES, PIECE, 128), BF16),
                pltpu.VMEM((PIECES, PIECE, 128), BF16),
                dma((5,)),
                dma((4,)),
                dma((4,)),
                dma((PIECES,)),
                dma((n,)),
                dma((PIECES,)),
                dma((n,)),
                dma((n,)),
                dma((PIECES,)),
                dma((n,)),
                dma((PIECES,)),
            ],
            compiler_params=pltpu.CompilerParams(
                collective_id=0, has_side_effects=True, vmem_limit_bytes=48 * 1024 * 1024
            ),
        )(
            snapshot.reshape(flat),
            cotangent.reshape(flat),
            first_weight,
            second_weight,
            face_codes,
        )
        return grad.reshape(snapshot.shape), up1, up2

    return jax.shard_map(
        body,
        mesh=mesh,
        in_specs=(
            P("groups", "blocks", None, None),
            P("groups", "blocks", None, None),
            P(),
            P(),
            P(("groups", "blocks"), None),
        ),
        out_specs=(P("groups", "blocks", None, None), P("groups", None), P("groups", None)),
        check_vma=False,
    )
```

time: 37.7 us -> 37 us (0.981)
  Pallas kernels: 30.5 us -> 29.8 us
    pallas_call x1, Pallas kernels: 30.5 us -> 29.8 us  [body(): pl.pallas_call(functools.partial(kernel, n, vertical), out_shape=(jax.Sha...]
where the time goes in v2:
time: 37 us; the launch traced here: 36.8 us
  Pallas kernels  29.8 us (81%)
  local copies, waits for them, and re-layouts  6.27 us (17%)
  between operations  0.65 us (2%)
    pallas_call x1, Pallas kernels, body(): pl.pallas_call(functools.partial(kernel, n, vertical), out_shape=(jax.Sha...  29.8 us
    unnamed x13, local copies, waits for them, and re-layouts  6.27 us

profile of v2, /device:TPU:0, one launch (start us, length us, event | category | flops | bytes accessed | tf_op | source)
XLA Modules:
  0.0 36.8 jit_solution(10623143299384621276)
XLA Ops:
  0.6 0.0 copy-start.4
  0.6 0.6 %copy-done.4 = s32[1,2]{1,0:T(1,128)S(1)} copy-done((s32[1,2]{1,0:T(1,128)S(1)}, s32[1,2]{1,0:T(1,128)}, u32[]{:S(2)}) %copy-start.4) | copy-done | bytes 32
  1.3 0.0 copy-start
  1.3 0.9 %copy-done = bf16[1,8,32,512]{3,2,1,0:T(8,128)(2,1)S(1)} copy-done((bf16[1,8,32,512]{3,2,1,0:T(8,128)(2,1)S(1)}, bf16[1,8,32,512]{3,2,1,0:T(8,128)(2,1)}, u32[]{:S(2)}) %copy-start) | copy-done | bytes 262168
  2.2 0.0 copy-start.1
  2.2 0.9 %copy-done.1 = bf16[1,8,32,512]{3,2,1,0:T(8,128)(2,1)S(1)} copy-done((bf16[1,8,32,512]{3,2,1,0:T(8,128)(2,1)S(1)}, bf16[1,8,32,512]{3,2,1,0:T(8,128)(2,1)}, u32[]{:S(2)}) %copy-start.1) | copy-done | bytes 262168
  3.2 0.0 copy-start.2
  3.2 0.8 %copy-done.2 = bf16[32,864]{1,0:T(8,128)(2,1)S(1)} copy-done((bf16[32,864]{1,0:T(8,128)(2,1)S(1)}, bf16[32,864]{1,0:T(8,128)(2,1)}, u32[]{:S(2)}) %copy-start.2) | copy-done | bytes 55320
  4.0 0.0 copy-start.3
  4.0 0.8 %copy-done.3 = bf16[32,864]{1,0:T(8,128)(2,1)S(1)} copy-done((bf16[32,864]{1,0:T(8,128)(2,1)S(1)}, bf16[32,864]{1,0:T(8,128)(2,1)}, u32[]{:S(2)}) %copy-start.3) | copy-done | bytes 55320
  4.8 29.8 %shard_map.76 = (f32[256,512]{1,0:T(8,128)S(1)}, f32[32,864]{1,0:T(8,128)S(1)}, f32[32,864]{1,0:T(8,128)S(1)}) custom-call(bf16[256,512]{1,0:T(8,128)(2,1)S(1)} %bitcast.4, bf16[256,512]{1,0:T(8,128)(2,1)S(1)} %bitcast.5, bf16[32,864]{1,0:T(8,128)(2,1)S(1)} %copy-done.2, bf16[32,864]{1,0:T(8,128)(2,1)S(1)} %copy-done.3, s32[1,2]{1,0:T(1,128)S(1)} %copy-done.4), custom_call_target="tpu_custom_call" | custom-call | tf_op jit(solution)/shard_map/pallas_call | solution.py:427
  34.7 0.8 %copy.11 = f32[1,8,32,512]{3,2,1,0:T(8,128)} copy(f32[1,8,32,512]{3,2,1,0:T(8,128)S(1)} %bitcast.3) | data formatting | bytes 1048576
  35.5 0.6 %copy.12 = f32[32,864]{1,0:T(8,128)} copy(f32[32,864]{1,0:T(8,128)S(1)} %get-tuple-element.13) | data formatting | bytes 221184
  36.1 0.6 %copy.13 = f32[32,864]{1,0:T(8,128)} copy(f32[32,864]{1,0:T(8,128)S(1)} %get-tuple-element.14) | data formatting | bytes 221184
Async XLA Ops:
  0.6 0.7 %copy-start.4 = (s32[1,2]{1,0:T(1,128)S(1)}, s32[1,2]{1,0:T(1,128)}, u32[]{:S(2)}) copy-start(s32[1,2]{1,0:T(1,128)} %codes_in.1) | copy-start | bytes 28
  1.3 0.9 %copy-start = (bf16[1,8,32,512]{3,2,1,0:T(8,128)(2,1)S(1)}, bf16[1,8,32,512]{3,2,1,0:T(8,128)(2,1)}, u32[]{:S(2)}) copy-start(bf16[1,8,32,512]{3,2,1,0:T(8,128)(2,1)} %param.5) | copy-start | bytes 786436
  2.2 0.9 %copy-start.1 = (bf16[1,8,32,512]{3,2,1,0:T(8,128)(2,1)S(1)}, bf16[1,8,32,512]{3,2,1,0:T(8,128)(2,1)}, u32[]{:S(2)}) copy-start(bf16[1,8,32,512]{3,2,1,0:T(8,128)(2,1)} %param.6) | copy-start | bytes 786436
  3.2 0.8 %copy-start.2 = (bf16[32,864]{1,0:T(8,128)(2,1)S(1)}, bf16[32,864]{1,0:T(8,128)(2,1)}, u32[]{:S(2)}) copy-start(bf16[32,864]{1,0:T(8,128)(2,1)} %w1_in.1) | copy-start | bytes 165892
  4.0 0.8 %copy-start.3 = (bf16[32,864]{1,0:T(8,128)(2,1)S(1)}, bf16[32,864]{1,0:T(8,128)(2,1)}, u32[]{:S(2)}) copy-start(bf16[32,864]{1,0:T(8,128)(2,1)} %w2_in.1) | copy-start | bytes 165892

commit v3 on v2

--- a/solution.py
+++ b/solution.py
@@ -115,17 +115,29 @@
             jnp.where(flip_z, tap(da, r, 2 - z), tap(da, r, z)),
         )
 
-    def block(x, columns, dr):
-        value = jnp.zeros((CH, 128), F32)
-        for index, column in enumerate(columns):
-            if column is None:
-                continue
-            y, dz = column
-            da = x - y + 1
-            if 0 <= da <= 2:
-                source = turned(da, dr, dz) if y in HALO else tap(da, dr, dz)
-                value = jnp.where(lane_block == index, source, value)
-        return value.astype(BF16)
+    def blocks_of(dr):
+        made = {}
+
+        def source(da, dz, halo_plane):
+            key = (da, dz, halo_plane)
+            if key not in made:
+                made[key] = turned(da, dr, dz) if halo_plane else tap(da, dr, dz)
+            return made[key]
+
+        def block(x, columns):
+            parts = tuple(
+                (index, x - column[0] + 1, column[1], column[0] in HALO)
+                for index, column in enumerate(columns)
+                if column is not None and 0 <= x - column[0] + 1 <= 2
+            )
+            if parts not in made:
+                value = jnp.zeros((CH, 128), F32)
+                for index, da, dz, halo_plane in parts:
+                    value = jnp.where(lane_block == index, source(da, dz, halo_plane), value)
+                made[parts] = value.astype(BF16)
+            return made[parts]
+
+        return block
 
     def plane_tiles(dz):
         return [[(y, dz) for y in group] for group in (INNER[:4], INNER[4:], HALO)]
@@ -138,44 +150,45 @@
     def fill(ref, lead, row, tile, value):
         ref[lead, pl.ds(row * CH, CH), pl.ds(tile * 128, 128)] = value
 
-    def build_main(dr, main):
+    def build_main(block, dr, main):
         for dz in range(3):
             for row, x in enumerate(INNER):
                 for tile in range(2):
-                    fill(main, 3 * dr + dz, row, tile, block(x, plane_tiles(dz)[tile], dr))
-
-    def build_forward(dr, side, edge):
+                    fill(main, 3 * dr + dz, row, tile, block(x, plane_tiles(dz)[tile]))
+
+    def build_forward(block, dr, side, edge):
         row = 0
         for dz in range(3):
             for x in HALO:
                 for tile in range(3):
-                    fill(side, dr, row, tile, block(x, plane_tiles(dz)[tile], dr))
+                    fill(side, dr, row, tile, block(x, plane_tiles(dz)[tile]))
                 row += 1
         row = 0
         for dz in range(3):
             for x in (0, 7):
-                fill(edge, dr, row, 0, block(x, plane_tiles(dz)[2], dr))
+                fill(edge, dr, row, 0, block(x, plane_tiles(dz)[2]))
                 row += 1
         for row in (6, 7):
             fill(edge, dr, row, 0, jnp.zeros((CH, 128), BF16))
 
-    def build_backward(dr, side, edge, planes):
+    def build_backward(block, dr, side, edge, planes):
         for row, x in enumerate(planes):
             for moved in range(3):
-                fill(side, dr, row, moved, block(x, plane_tiles(2 - moved)[2], dr))
+                fill(side, dr, row, moved, block(x, plane_tiles(2 - moved)[2]))
         if edge is not None:
             for row, x in enumerate(HALO):
-                fill(edge, dr, row, 0, block(x, [(0, 2), (7, 2), (0, 1), (7, 1)], dr))
-                fill(edge, dr, row, 1, block(x, [(0, 0), (7, 0), None, None], dr))
+                fill(edge, dr, row, 0, block(x, [(0, 2), (7, 2), (0, 1), (7, 1)]))
+                fill(edge, dr, row, 1, block(x, [(0, 0), (7, 0), None, None]))
 
     def shifts(value):
         rows, lanes = value.shape
-        z = lax.broadcasted_iota(jnp.int32, (rows, lanes), 0) % vertical
-        return [
-            jnp.where(z == 0, 0.0, pltpu.roll(value, 1, 0)),
-            value,
-            jnp.where(z == vertical - 1, 0.0, pltpu.roll(value, rows - 1, 0)),
-        ]
+        z = lax.broadcasted_iota(jnp.int32, (1, vertical, lanes), 1)
+
+        def moved(steps, outside):
+            grid = pltpu.roll(value, steps % rows, 0).reshape(rows // vertical, vertical, lanes)
+            return jnp.where(z == outside, 0.0, grid).reshape(rows, lanes)
+
+        return [moved(1, 0), value, moved(-1, vertical - 1)]
 
     inside = pl.ds(vertical, cells)
 
@@ -199,9 +212,10 @@
     spread_taps(w1_ref)
 
     def build1(dr, carry):
-        build_main(dr, main1)
-        build_forward(dr, side1, edge1)
-        build_backward(dr, back1, None, INNER)
+        block = blocks_of(dr)
+        build_main(block, dr, main1)
+        build_forward(block, dr, side1, edge1)
+        build_backward(block, dr, back1, None, INNER)
         return carry
 
     lax.fori_loop(0, 3, build1, 0)
@@ -212,8 +226,9 @@
     spread_taps(w2_ref)
 
     def build2(dr, carry):
-        build_main(dr, main2)
-        build_backward(dr, side2, edge2, INNER + HALO)
+        block = blocks_of(dr)
+        build_main(block, dr, main2)
+        build_backward(block, dr, side2, edge2, INNER + HALO)
         return carry
 
     lax.fori_loop(0, 3, build2, 0)
@@ -279,7 +294,7 @@
             for dz in range(3):
                 full = nn(left, field[dz, up(dr), :])
                 for da in range(3):
-                    total = None
+                    places = [None] * 4
                     for a in range(PLANES):
                         tile, place = lane_place(a + da - 1)
                         if tile == 2:
@@ -287,16 +302,29 @@
                             piece = outer[row : row + CH, dz * 128 : (dz + 1) * 128]
                         else:
                             piece = full[a * CH : (a + 1) * CH, tile * 128 : (tile + 1) * 128]
-                        total = added(total, jnp.where(lane_block == place, piece, 0.0))
-                    total = total + pltpu.roll(total, 64, 1)
-                    total = total + pltpu.roll(total, 32, 1)
+                        places[place] = added(places[place], piece)
+                    total = jnp.where(
+                        lane_block < 2,
+                        jnp.where(lane_block == 0, places[0], places[1]),
+                        jnp.where(lane_block == 2, places[2], places[3]),
+                    )
                     found[9 * da + 3 * dr + dz] = total
+        found[27] = jnp.zeros((CH, 128), F32)
+        half = lane_block < 2
+        even = lane_block % 2 == 0
+
+        def join(first, second, mask, steps):
+            return jnp.where(mask, first, second) + pltpu.roll(
+                jnp.where(mask, second, first), steps, 1
+            )
+
         for tile in range(7):
-            value = jnp.zeros((CH, 128), F32)
-            for place in range(4):
-                if 4 * tile + place < 27:
-                    value = jnp.where(lane_block == place, found[4 * tile + place], value)
-            result[pl.ds(tile * CH, CH), :] = value
+            t0, t1, t2, t3 = (found[4 * tile + place] for place in range(4))
+            low_pair, high_pair = join(t0, t2, half, 64), join(t1, t3, half, 64)
+            left = jnp.where(even, low_pair, high_pair)
+            right_even = pltpu.roll(low_pair, 96, 1)
+            right_odd = pltpu.roll(high_pair, 32, 1)
+            result[pl.ds(tile * CH, CH), :] = left + jnp.where(even, right_even, right_odd)
 
     def scatter_copy(grad, slots, send, recv, owner, source):
         return pltpu.make_async_remote_copy(
@@ -481,7 +509,7 @@
                 dma((PIECES,)),
             ],
             compiler_params=pltpu.CompilerParams(
-                collective_id=0, has_side_effects=True, vmem_limit_bytes=48 * 1024 * 1024
+                collective_id=0, has_side_effects=True, vmem_limit_bytes=63 * 1024 * 1024
             ),
         )(
             snapshot.reshape(flat),

time: 37 us -> 35.2 us (0.951)
  local copies, waits for them, and re-layouts: 6.27 us -> 3.49 us
  Pallas kernels: 29.8 us -> 30.9 us
    unnamed x13 -> x7, local copies, waits for them, and re-layouts: 6.27 us -> 3.49 us
    pallas_call x1, Pallas kernels: 29.8 us -> 30.9 us  [body(): pl.pallas_call(functools.partial(kernel, n, vertical), out_shape=(jax.Sha...]
where the time goes in v3:
time: 35.2 us; the launch traced here: 35.1 us
  Pallas kernels  30.9 us (88%)
  local copies, waits for them, and re-layouts  3.49 us (10%)
  between operations  0.65 us (2%)
    pallas_call x1, Pallas kernels, body(): pl.pallas_call(functools.partial(kernel, n, vertical), out_shape=(jax.Sha...  30.9 us
    unnamed x7, local copies, waits for them, and re-layouts  3.49 us

profile of v3, /device:TPU:0, one launch (start us, length us, event | category | flops | bytes accessed | tf_op | source)
XLA Modules:
  0.0 35.1 jit_solution(9368757418105373058)
XLA Ops:
  0.6 30.9 %shard_map.76 = (f32[256,512]{1,0:T(8,128)}, f32[32,864]{1,0:T(8,128)}, f32[32,864]{1,0:T(8,128)}) custom-call(bf16[256,512]{1,0:T(8,128)(2,1)} %bitcast.4, bf16[256,512]{1,0:T(8,128)(2,1)} %bitcast.5, bf16[32,864]{1,0:T(8,128)(2,1)} %w1_in.1, bf16[32,864]{1,0:T(8,128)(2,1)} %w2_in.1, s32[1,2]{1,0:T(1,128)} %codes_in.1), custom_call_target="tpu_custom_call" | custom-call | tf_op jit(solution)/shard_map/pallas_call | solution.py:455
  31.6 0.0 copy-start.1
  31.6 1.9 %copy.11 = f32[1,8,32,512]{3,2,1,0:T(8,128)} copy(f32[1,8,32,512]{3,2,1,0:T(8,128)} %bitcast.3) | data formatting | bytes 1048576
  33.5 0.0 copy-done.1
  33.5 0.0 copy-start
  33.5 0.6 %copy.12 = f32[32,864]{1,0:T(8,128)} copy(f32[32,864]{1,0:T(8,128)S(1)} %copy-done.1) | data formatting | bytes 221184
  34.1 0.3 copy-done
  34.4 0.6 %copy.13 = f32[32,864]{1,0:T(8,128)} copy(f32[32,864]{1,0:T(8,128)S(1)} %copy-done) | data formatting | bytes 221184
Async XLA Ops:
  31.6 1.9 %copy-start.1 = (f32[32,864]{1,0:T(8,128)S(1)}, f32[32,864]{1,0:T(8,128)}, u32[]{:S(2)}) copy-start(f32[32,864]{1,0:T(8,128)} %get-tuple-element.13) | copy-start | bytes 331780
  33.5 0.9 %copy-start = (f32[32,864]{1,0:T(8,128)S(1)}, f32[32,864]{1,0:T(8,128)}, u32[]{:S(2)}) copy-start(f32[32,864]{1,0:T(8,128)} %get-tuple-element.14) | copy-start | bytes 331780
